TPU v7x, 32 devices: a whole 2x2x4 slice. The times are simulated.
32 devices in a mesh: dp: 4 (over z), tensor: 8 (over y, x, core).
Axes of the slice: x: 2, y: 2, z: 4, core: 2. Of those that a mesh axis runs over, the one named last changes fastest.
Arguments:
- image_rows: bfloat16 [256, 4, 4096], P('tensor', 'dp'), may hold values from -6 to 6
- text_rows: bfloat16 [256, 4, 4096], P('tensor', 'dp'), may hold values from -6 to 6
- text_count: int32 [4], P('dp'), may hold values from 64 to 256, as said below
- slot_kind: int32 [4], replicated, may hold values from 0 to 1, as said below
- attn_gain: float32 [4096], replicated, may hold values from 0.1 to 1.9
- qkv_weight: bfloat16 [4096, 3, 4096], P(None, None, 'tensor'), may hold values from -1 to 1
- out_weight: bfloat16 [4096, 4096], P('tensor'), may hold values from -0.09375 to 0.09375
- expert_gain: float32 [4, 4096], P('dp'), may hold values from 0.1 to 1.9
- expert_in: bfloat16 [4, 4096, 16384], P('dp', None, 'tensor'), may hold values from -0.09375 to 0.09375
- expert_out: bfloat16 [4, 16384, 4096], P('dp', 'tensor'), may hold values from -0.046875 to 0.046875
Outputs:
- image_out: bfloat16 [256, 4, 4096], P('tensor', 'dp')
- text_out: bfloat16 [256, 4, 4096], P('tensor', 'dp')
Inputs may be any that keep to these rules, and one draw needn't show every extreme that they name: For each pair the first text_count text slots are live; some pair has 256 and some pair 256 // 4 live text slots. `slot_kind`: exactly 1 of the 4 slots serve one modality (which one is drawn), the rest serve the other, so that one slot receives rows from 4 dp indices.
All inputs are finite; a program needn't handle non-finite values.
Results may differ from a plain program's by a relative error of at most 0.015.
Values may be sent and summed in bfloat16 or wider, within the bound.
A program may use at most 192 MiB of HBM per device.

v0:
```python
import jax
import jax.numpy as jnp
from jax import lax
from jax.sharding import PartitionSpec as P

HDIM = 128
CAP = 4


def layer_norm(values, gain):
    floats = values.astype(jnp.float32)
    center = floats - jnp.mean(floats, axis=-1, keepdims=True)
    spread = jnp.mean(center * center, axis=-1, keepdims=True)
    return center * lax.rsqrt(spread + 1e-05) * gain


def route_slot(slot_kind, kind, source):
    member = (slot_kind == kind).astype(jnp.int32)
    member_count = jnp.sum(member)
    member_rank = jnp.cumsum(member) - member
    target = source % member_count
    slot_ids = jnp.arange(slot_kind.shape[0], dtype=jnp.int32)
    picked = jnp.where((member == 1) & (member_rank == target), slot_ids, 0)
    return jnp.sum(picked)


def body(
    image_rows,
    text_rows,
    text_count,
    slot_kind,
    attn_gain,
    qkv_weight,
    out_weight,
    expert_gain,
    expert_in,
    expert_out,
):
    row_count = image_rows.shape[0]
    pair_count = image_rows.shape[1]
    model_width = image_rows.shape[2]
    tensor_size = lax.axis_size("tensor")
    slot_rows = row_count * tensor_size
    tensor_place = lax.axis_index("tensor")
    dp_place = lax.axis_index("dp")
    head_local = qkv_weight.shape[2] // HDIM
    stacked = jnp.stack([image_rows, text_rows], axis=0)
    normed = layer_norm(stacked, attn_gain).astype(jnp.bfloat16)
    qkv_flat = qkv_weight.reshape(model_width, -1)
    mixed = jnp.einsum(
        "mrpd,dk->mrpk",
        lax.all_gather(normed, "tensor", axis=1, tiled=True),
        qkv_flat,
        preferred_element_type=jnp.float32,
    ).astype(jnp.bfloat16)
    mixed = mixed.reshape(2 * slot_rows, pair_count, 3, head_local, HDIM)
    queries = mixed[:, :, 0]
    keys_all = mixed[:, :, 1]
    values_all = mixed[:, :, 2]
    scores = jnp.einsum(
        "qphk,sphk->phqs", queries, keys_all, preferred_element_type=jnp.float32
    ) * HDIM ** (-0.5)
    positions = jnp.arange(2 * slot_rows, dtype=jnp.int32)
    key_live = (positions[None, :] < slot_rows) | (
        positions[None, :] - slot_rows < text_count[:, None]
    )
    scores = jnp.where(key_live[:, None, None, :], scores, -1e30)
    scores = scores - jnp.max(scores, axis=-1, keepdims=True)
    weights = jnp.exp(scores)
    weights = (weights / jnp.sum(weights, axis=-1, keepdims=True)).astype(jnp.bfloat16)
    context = jnp.einsum(
        "phqs,sphk->qphk", weights, values_all, preferred_element_type=jnp.float32
    ).astype(jnp.bfloat16)
    context = context.reshape(2, slot_rows, pair_count, head_local * HDIM)
    terms = jnp.einsum("mspk,kd->smpd", context, out_weight, preferred_element_type=jnp.float32)
    attended = lax.psum_scatter(
        terms.astype(jnp.bfloat16), "tensor", scatter_dimension=0, tiled=True
    ).astype(jnp.float32)
    image_hidden = (image_rows.astype(jnp.float32) + attended[:, 0]).astype(jnp.bfloat16)
    text_hidden = (text_rows.astype(jnp.float32) + attended[:, 1]).astype(jnp.bfloat16)
    slot_total = slot_kind.shape[0]
    slot_ids = jnp.arange(slot_total, dtype=jnp.int32)
    image_dest = route_slot(slot_kind, 0, dp_place)
    text_dest = route_slot(slot_kind, 1, dp_place)
    chosen = slot_ids[None, :, None, None]
    nothing = jnp.zeros((row_count, slot_total, pair_count, model_width), jnp.bfloat16)
    outgoing = jnp.where(
        chosen == image_dest,
        image_hidden[:, None],
        jnp.where(chosen == text_dest, text_hidden[:, None], nothing),
    )
    arrived = lax.all_to_all(outgoing, "dp", split_axis=1, concat_axis=1, tiled=True)
    own_kind = slot_kind[dp_place]
    member = (slot_kind == own_kind).astype(jnp.int32)
    member_count = jnp.sum(member)
    own_rank = jnp.sum(jnp.where(slot_ids < dp_place, member, 0))
    sender_ids = own_rank + jnp.arange(CAP, dtype=jnp.int32) * member_count
    sender_live = sender_ids < slot_total
    sender_clip = jnp.minimum(sender_ids, slot_total - 1)
    packed = jnp.take(arrived, sender_clip, axis=1)
    packed = jnp.where(sender_live[None, :, None, None], packed, jnp.zeros_like(packed))
    gathered = lax.all_gather(packed, "tensor", axis=0, tiled=True)
    own_gain = expert_gain[0]
    own_in = expert_in[0]
    own_out = expert_out[0]
    scaled = layer_norm(gathered, own_gain).astype(jnp.bfloat16)
    inner = jnp.einsum("scpd,df->scpf", scaled, own_in, preferred_element_type=jnp.float32)
    inner = jax.nn.gelu(inner, approximate=False).astype(jnp.bfloat16)
    expert_rows_out = lax.psum_scatter(
        jnp.einsum("scpf,fd->scpd", inner, own_out, preferred_element_type=jnp.float32).astype(
            jnp.bfloat16
        ),
        "tensor",
        scatter_dimension=0,
        tiled=True,
    )
    back_live = slot_ids % member_count == own_rank
    back_index = jnp.minimum(slot_ids // member_count, CAP - 1)
    going_back = jnp.take(expert_rows_out, back_index, axis=1)
    going_back = jnp.where(back_live[None, :, None, None], going_back, jnp.zeros_like(going_back))
    returned = lax.all_to_all(going_back, "dp", split_axis=1, concat_axis=1, tiled=True)
    image_ffn = lax.dynamic_index_in_dim(returned, image_dest, 1, keepdims=False)
    text_ffn = lax.dynamic_index_in_dim(returned, text_dest, 1, keepdims=False)
    image_out = (image_hidden.astype(jnp.float32) + image_ffn.astype(jnp.float32)).astype(
        jnp.bfloat16
    )
    text_sum = (text_hidden.astype(jnp.float32) + text_ffn.astype(jnp.float32)).astype(jnp.bfloat16)
    slot_index = tensor_place * row_count + jnp.arange(row_count, dtype=jnp.int32)
    live = slot_index[:, None, None] < text_count[None, :, None]
    text_out = jnp.where(live, text_sum, jnp.zeros_like(text_sum))
    return (image_out, text_out)


def solution(mesh):
    return jax.shard_map(
        body,
        mesh=mesh,
        in_specs=(
            P("tensor", "dp", None),
            P("tensor", "dp", None),
            P("dp"),
            P(),
            P(),
            P(None, None, "tensor"),
            P("tensor", None),
            P("dp", None),
            P("dp", None, "tensor"),
            P("dp", "tensor", None),
        ),
        out_specs=(P("tensor", "dp", None), P("tensor", "dp", None)),
        check_vma=False,
    )
```

profile of v0, /device:TPU:0, one launch (start us, length us, event | category | flops | bytes accessed | tf_op | source)
XLA Modules:
  0.0 419.8 jit_solution(4326660846055092674)
XLA Ops:
  7.2 1.2 convert_reduce_fusion.1
  8.4 1.3 fusion.76
  9.8 2.1 fusion.78
  11.9 17.0 %copy.18 = bf16[4096,3,512]{0,2,1:T(8,128)(2,1)} copy(bf16[4096,3,512]{2,0,1:T(8,128)(2,1)} %param.17) | data formatting | bytes 25165824 | tf_op args[5]
  29.5 21.9 %all-gather.3.cloned.1.call-done = bf16[2,256,1,4096]{3,1,0,2:T(8,128)(2,1)} async-done(((bf16[2,32,1,4096]{3,1,0,2:T(8,128)(2,1)}), bf16[2,256,1,4096]{3,1,0,2:T(8,128)(2,1)}) %all-gather.3.cloned.1.call-update) | async-done | bytes 4194320 | tf_op jit(solution)/shard_map/all_gather | solution.py:52
  51.4 11.9 %fusion.63 = bf16[2,256,1536]{2,1,0:T(8,128)(2,1)} fusion(bf16[4096,1536,1]{0,1,2:T(8,128)(2,1)} %bitcast.123, bf16[2,256,1,4096]{3,1,0,2:T(8,128)(2,1)} %all-gather.3.cloned.1.call-done), kind=kOutput, calls=%fused_computation.81 | convolution fusion | flops 6443237376 | bytes 18350080 | tf_op jit(solution)/shard_map/mrpd,dk->mrpk/dot_general | solution.py:50
  63.3 3.0 reshape.442
  67.9 1.4 fusion.140
  69.9 6.5 %fusion.26 = bf16[256,2,1,4096]{3,0,1,2:T(8,128)(2,1)} fusion(bf16[512,4096]{1,0:T(8,128)(2,1)} %param.18, bf16[2,256,512]{1,0,2:T(2,128)(2,1)S(1)} %reshape.446), kind=kOutput, calls=%fused_computation.42 | convolution fusion | flops 2149580800 | bytes 8912896 | tf_op jit(solution)/shard_map/mspk,kd->smpd/dot_general | solution.py:75
  77.1 1.4 fusion.94
  82.0 1.2 iota_compare_fusion.1
  83.2 44.7 %reduce-scatter.3.cloned.1.call-done = bf16[32,2,1,4096]{3,0,1,2:T(8,128)(2,1)} async-done(((bf16[256,2,1,4096]{3,0,1,2:T(8,128)(2,1)}), bf16[32,2,1,4096]{3,0,1,2:T(8,128)(2,1)}) %reduce-scatter.3.cloned.1.call-update) | async-done | bytes 524304 | tf_op jit(solution)/shard_map/reduce_scatter | solution.py:76
  128.0 1.2 convert_bitcast_fusion.1
  130.3 1.2 select_select_fusion
  131.5 4.6 %all-to-all-start = ((bf16[32,4,1,4096]{3,0,2,1:T(8,128)(2,1)}), bf16[32,4,1,4096]{3,0,2,1:T(8,128)(2,1)S(1)}, u32[]{:S(2)}, u32[]{:S(2)}) async-start(bf16[32,4,1,4096]{3,0,2,1:T(8,128)(2,1)} %select_select_fusion), calls=%async_computation.1 | async-start | bytes 2097152 | tf_op jit(solution)/shard_map/all_to_all | solution.py:92
  136.1 1.3 compare_and_fusion.1
  137.4 24.4 %all-to-all-done = bf16[32,4,1,4096]{3,0,2,1:T(8,128)(2,1)S(1)} async-done(((bf16[32,4,1,4096]{3,0,2,1:T(8,128)(2,1)}), bf16[32,4,1,4096]{3,0,2,1:T(8,128)(2,1)S(1)}, u32[]{:S(2)}, u32[]{:S(2)}) %all-to-all-start) | async-done | bytes 1048608 | tf_op jit(solution)/shard_map/all_to_all | solution.py:92
  161.8 1.7 gather_fusion
  163.5 2.5 fusion.82
  166.3 52.3 %all-gather.5.cloned.1.call-done = bf16[256,4,1,4096]{3,0,2,1:T(8,128)(2,1)} async-done(((bf16[32,4,1,4096]{3,0,2,1:T(8,128)(2,1)}), bf16[256,4,1,4096]{3,0,2,1:T(8,128)(2,1)}) %all-gather.5.cloned.1.call-update) | async-done | bytes 8388624 | tf_op jit(solution)/shard_map/all_gather | solution.py:102
  218.6 4.7 %convert_reduce_fusion = f32[256,4]{0,1:T(4,128)S(1)} fusion(bf16[256,4,1,4096]{3,0,2,1:T(8,128)(2,1)} %all-gather.5.cloned.1.call-done), kind=kLoop, calls=%fused_computation.4 | loop fusion | flops 8387584 | bytes 8392704 | tf_op jit(solution)/shard_map/reduce_sum | solution.py:12
  223.4 1.1 copy-done
  224.4 2.3 fusion.3
  226.7 24.4 %fusion.70 = (u8[256,2048]{1,0:T(8,128)(4,1)S(1)}, u8[256,2048]{1,0:T(8,128)(4,1)S(1)}, f32[256,4,2048]{2,0,1:T(8,128)}) fusion(bf16[1,4096,2048]{2,1,0:T(8,128)(2,1)} %param.20, bf16[256,4,1,4096]{3,0,2,1:T(8,128)(2,1)S(1)} %copy-done, f32[4096]{0:T(1024)S(1)} %bitcast.132, f32[256,4]{0,1:T(4,128)S(1)} %add_rsqrt_fusion, ...), kind=kOutput, calls=%fused_computation.86 | convolution fusion | flops 17227055104 | bytes 34627584 | tf_op jit(solution)/shard_map/scpd,df->scpf/dot_general | solution.py:107
  251.2 54.5 %convert_bitcast_fusion = bf16[256,4,1,4096]{3,0,1,2:T(8,128)(2,1)} fusion(bf16[1,2048,4096]{2,1,0:T(8,128)(2,1)} %param.21, f32[256,4,2048]{2,0,1:T(8,128)} %get-tuple-element.24, u8[256,2048]{1,0:T(8,128)(4,1)S(1)} %get-tuple-element.4, u8[256,2048]{1,0:T(8,128)(4,1)S(1)} %get-tuple-element.3), kind=kOutput, calls=%fused_computation.24 | convolution fusion | flops 17330864128 | bytes 34603008 | tf_op jit(solution)/shard_map/scpf,fd->scpd/dot_general | solution.py:110
  307.8 1.5 compare_and_fusion
  309.3 67.9 %reduce-scatter.5.cloned.1.call-done = bf16[32,4,1,4096]{3,0,1,2:T(8,128)(2,1)} async-done(((bf16[256,4,1,4096]{3,0,1,2:T(8,128)(2,1)}), bf16[32,4,1,4096]{3,0,1,2:T(8,128)(2,1)}) %reduce-scatter.5.cloned.1.call-update) | async-done | bytes 1048592 | tf_op jit(solution)/shard_map/reduce_scatter | solution.py:109
  377.1 1.8 gather_fusion.1
  379.0 1.2 fusion.81
  380.2 4.6 %all-to-all-start.1 = ((bf16[32,4,1,4096]{3,0,2,1:T(8,128)(2,1)}), bf16[32,4,1,4096]{3,0,2,1:T(8,128)(2,1)S(1)}, u32[]{:S(2)}, u32[]{:S(2)}) async-start(bf16[32,4,1,4096]{3,0,2,1:T(8,128)(2,1)} %fusion.81), calls=%async_computation.3 | async-start | bytes 2097152 | tf_op jit(solution)/shard_map/all_to_all | solution.py:121
  388.4 22.1 %all-to-all-done.1 = bf16[32,4,1,4096]{3,0,2,1:T(8,128)(2,1)S(1)} async-done(((bf16[32,4,1,4096]{3,0,2,1:T(8,128)(2,1)}), bf16[32,4,1,4096]{3,0,2,1:T(8,128)(2,1)S(1)}, u32[]{:S(2)}, u32[]{:S(2)}) %all-to-all-start.1) | async-done | bytes 1048608 | tf_op jit(solution)/shard_map/all_to_all | solution.py:121
  411.3 1.8 fusion.92
  (39 shorter events, 6.1 us)
Async XLA Ops:
  7.2 44.3 %all-gather.3.cloned.1.call-start = ((), (), s32[]{:S(2)}) async-start(), calls=%async_computation.4 | async-start | bytes 4718592 | tf_op jit(solution)/shard_map/all_gather | solution.py:52
  11.9 116.1 %reduce-scatter.3.cloned.1.call-start = ((), (), s32[]{:S(2)}) async-start(), calls=%async_computation.5 | async-start | bytes 4718592 | tf_op jit(solution)/shard_map/reduce_scatter | solution.py:76
  69.8 6.7 %copy-start.4 = (s32[4]{0:T(128)S(1)}, s32[4]{0:T(128)}, u32[]{:S(2)}) copy-start(s32[4]{0:T(128)} %param.15) | copy-start | bytes 52
  69.8 60.4 %copy-start.1 = (bf16[32,1,4096]{2,0,1:T(8,128)(2,1)S(1)}, bf16[32,1,4096]{2,0,1:T(8,128)(2,1)}, u32[]{:S(2)}) copy-start(bf16[32,1,4096]{2,0,1:T(8,128)(2,1)} %param.12) | copy-start | bytes 786436
  69.8 60.4 %copy-start.2 = (bf16[32,1,4096]{2,0,1:T(8,128)(2,1)S(1)}, bf16[32,1,4096]{2,0,1:T(8,128)(2,1)}, u32[]{:S(2)}) copy-start(bf16[32,1,4096]{2,0,1:T(8,128)(2,1)} %param.13) | copy-start | bytes 786436
  129.2 1.0 copy-start.3
  131.5 30.3 %all-to-all-start = ((bf16[32,4,1,4096]{3,0,2,1:T(8,128)(2,1)}), bf16[32,4,1,4096]{3,0,2,1:T(8,128)(2,1)S(1)}, u32[]{:S(2)}, u32[]{:S(2)}) async-start(bf16[32,4,1,4096]{3,0,2,1:T(8,128)(2,1)} %select_select_fusion), calls=%async_computation.1 | async-start | bytes 2097152 | tf_op jit(solution)/shard_map/all_to_all | solution.py:92
  136.1 82.6 %all-gather.5.cloned.1.call-start = ((), (), s32[]{:S(2)}) async-start(), calls=%async_computation.6 | async-start | bytes 9437184 | tf_op jit(solution)/shard_map/all_gather | solution.py:102
  166.0 60.8 %copy-start.5 = (f32[1,4096]{1,0:T(1,128)S(1)}, f32[1,4096]{1,0:T(1,128)}, u32[]{:S(2)}) copy-start(f32[1,4096]{1,0:T(1,128)} %param.19) | copy-start | bytes 49156
  166.0 211.2 %reduce-scatter.5.cloned.1.call-start = ((), (), s32[]{:S(2)}) async-start(), calls=%async_computation.7 | async-start | bytes 9437184 | tf_op jit(solution)/shard_map/reduce_scatter | solution.py:109
  218.6 5.8 %copy-start = (bf16[256,4,1,4096]{3,0,2,1:T(8,128)(2,1)S(1)}, bf16[256,4,1,4096]{3,0,2,1:T(8,128)(2,1)}, u32[]{:S(2)}) copy-start(bf16[256,4,1,4096]{3,0,2,1:T(8,128)(2,1)} %all-gather.5.cloned.1.call-done) | copy-start | bytes 25165828
  380.2 30.3 %all-to-all-start.1 = ((bf16[32,4,1,4096]{3,0,2,1:T(8,128)(2,1)}), bf16[32,4,1,4096]{3,0,2,1:T(8,128)(2,1)S(1)}, u32[]{:S(2)}, u32[]{:S(2)}) async-start(bf16[32,4,1,4096]{3,0,2,1:T(8,128)(2,1)} %fusion.81), calls=%async_computation.3 | async-start | bytes 2097152 | tf_op jit(solution)/shard_map/all_to_all | solution.py:121
Sparse Core Ops, SparseCore 0:
  12.0 39.4 all-gather.2
  76.6 51.3 reduce-scatter.2
  166.1 52.4 all-gather.4
  305.8 71.2 reduce-scatter.4
where the time goes:
time: 424 us; the launch traced here: 420 us
  waiting for transfers between devices  233 us (55%)
  matrix products  98.5 us (23%)
  other arithmetic  28.3 us (7%)
  local copies, waits for them, and re-layouts  27.1 us (6%)
  between operations  23 us (5%)
  starting transfers between devices  9.56 us (2%)
    reduce_scatter x1, waiting for transfers between devices, body(): lax.psum_scatter(jnp.einsum('scpf,fd->scpd', inner, own_out, preferred_el...  67.9 us
    dot_general x1, matrix products, body(): jnp.einsum('scpf,fd->scpd', inner, own_out, preferred_element_type=jnp.fl...  54.5 us
    all_gather x1, waiting for transfers between devices, body(): gathered = lax.all_gather(packed, 'tensor', axis=0, tiled=True)  52.3 us
    reduce_scatter x1, waiting for transfers between devices, body(): lax.psum_scatter(terms.astype(jnp.bfloat16), 'tensor', scatter_dimension=...  44.7 us
    dot_general x1, matrix products, body(): jnp.einsum('scpd,df->scpf', scaled, own_in, preferred_element_type=jnp.fl...  24.4 us
    all_to_all x1, waiting for transfers between devices, body(): lax.all_to_all(outgoing, 'dp', split_axis=1, concat_axis=1, tiled=True)  24.4 us
    all_to_all x1, waiting for transfers between devices, body(): lax.all_to_all(going_back, 'dp', split_axis=1, concat_axis=1, tiled=True)  22.1 us
    all_gather x1, waiting for transfers between devices, body(): lax.all_gather(normed, 'tensor', axis=1, tiled=True)  21.9 us
  transfers between devices with their start and end apart: 6, of which 6 were waited for; matrix products, arithmetic and copies ran while one was open for 6% of the time, Pallas kernels for 0%

commit v1 on v0

v1 whole, which is shorter than its diff:
```python
import functools

import jax
import jax.numpy as jnp
from jax import lax
from jax.experimental import pallas as pl
from jax.experimental.pallas import tpu as pltpu
from jax.sharding import PartitionSpec as P

HDIM = 128
CAP = 4
CHUNKS = 2


def layer_norm(values, gain):
    floats = values.astype(jnp.float32)
    center = floats - jnp.mean(floats, axis=-1, keepdims=True)
    spread = jnp.mean(center * center, axis=-1, keepdims=True)
    return center * lax.rsqrt(spread + 1e-05) * gain


def route_slot(slot_kind, kind, source):
    slot_ids = jnp.arange(slot_kind.shape[0], dtype=jnp.int32)
    member = (slot_kind == kind).astype(jnp.int32)
    member_count = jnp.sum(member)
    earlier = (slot_ids[None, :] < slot_ids[:, None]).astype(jnp.int32)
    member_rank = jnp.sum(earlier * member[None, :], axis=1)
    target = source % member_count
    picked = jnp.where((member == 1) & (member_rank == target), slot_ids, 0)
    return jnp.sum(picked)


def attention_kernel(heads, live_ref, q_ref, k_ref, v_ref, out_ref):
    live = live_ref[...] > 0
    for head in range(heads):
        columns = slice(head * HDIM, (head + 1) * HDIM)
        scores = lax.dot_general(
            q_ref[:, columns],
            k_ref[:, columns],
            (((1,), (1,)), ((), ())),
            preferred_element_type=jnp.float32,
        ) * HDIM ** (-0.5)
        scores = jnp.where(live, scores, -1e30)
        weights = jnp.exp(scores - jnp.max(scores, axis=-1, keepdims=True))
        weights = weights / jnp.sum(weights, axis=-1, keepdims=True)
        out_ref[:, columns] = jnp.dot(
            weights.astype(jnp.bfloat16), v_ref[:, columns], preferred_element_type=jnp.float32
        ).astype(jnp.bfloat16)


def attention(live, queries, keys, values):
    rows, width = queries.shape
    count = keys.shape[0]
    heads = width // HDIM
    return pl.pallas_call(
        functools.partial(attention_kernel, heads),
        out_shape=jax.ShapeDtypeStruct((rows, width), jnp.bfloat16),
        in_specs=[pl.BlockSpec(memory_space=pltpu.VMEM)] * 4,
        out_specs=pl.BlockSpec(memory_space=pltpu.VMEM),
        cost_estimate=pl.CostEstimate(
            flops=4 * rows * count * width,
            bytes_accessed=4 * (rows + count) * width,
            transcendentals=rows * count * heads,
        ),
        compiler_params=pltpu.CompilerParams(vmem_limit_bytes=24 * 2**20),
    )(live, queries, keys, values)


def matmul(left, right):
    return jnp.dot(left, right, preferred_element_type=jnp.float32)


def body(
    image_rows,
    text_rows,
    text_count,
    slot_kind,
    attn_gain,
    qkv_weight,
    out_weight,
    expert_gain,
    expert_in,
    expert_out,
):
    row_count = image_rows.shape[0]
    model_width = image_rows.shape[2]
    tensor_size = lax.axis_size("tensor")
    tensor_place = lax.axis_index("tensor")
    dp_place = lax.axis_index("dp")
    slot_total = slot_kind.shape[0]
    part = row_count // CHUNKS
    stacked = jnp.stack(
        [image_rows.reshape(row_count, model_width), text_rows.reshape(row_count, model_width)]
    )

    def rows_of(chunk):
        return stacked[:, chunk * part : (chunk + 1) * part]

    projected = []
    for chunk in range(CHUNKS):
        normed = layer_norm(rows_of(chunk), attn_gain).astype(jnp.bfloat16)
        gathered = lax.all_gather(normed, "tensor", axis=0).reshape(-1, model_width)
        projected.append(
            [matmul(gathered, qkv_weight[:, i]).astype(jnp.bfloat16) for i in range(3)]
        )
    keys = jnp.concatenate([p[1] for p in projected], axis=0)
    values = jnp.concatenate([p[2] for p in projected], axis=0)
    place = jnp.arange(CHUNKS * tensor_size * 2 * part, dtype=jnp.int32)
    key_chunk, rest = place // (tensor_size * 2 * part), place % (tensor_size * 2 * part)
    key_row = rest // (2 * part) * row_count + key_chunk * part + rest % part
    is_text = rest // part % 2
    live_keys = ((is_text == 0) | (key_row < text_count[0])).astype(jnp.int32)[None, :]

    image_dest = route_slot(slot_kind, 0, dp_place)
    text_dest = route_slot(slot_kind, 1, dp_place)
    slot_ids = jnp.arange(slot_total, dtype=jnp.int32)
    own_kind = lax.dynamic_index_in_dim(slot_kind, dp_place, 0, keepdims=False)
    member = (slot_kind == own_kind).astype(jnp.int32)
    member_count = jnp.sum(member)
    own_rank = jnp.sum(jnp.where(slot_ids < dp_place, member, 0))

    hiddens, arrivals = [], []
    for chunk in range(CHUNKS):
        context = attention(live_keys, projected[chunk][0], keys, values)
        terms = matmul(context, out_weight).astype(jnp.bfloat16)
        terms = terms.reshape(tensor_size, 2 * part, model_width)
        attended = lax.psum_scatter(terms, "tensor", scatter_dimension=0)
        attended = attended.reshape(2, part, model_width).astype(jnp.float32)
        hidden = (rows_of(chunk).astype(jnp.float32) + attended).astype(jnp.bfloat16)
        hiddens.append(hidden)
        outgoing = jnp.where((slot_kind == 0)[:, None, None], hidden[0][None], hidden[1][None])
        arrivals.append(lax.all_to_all(outgoing, "dp", split_axis=0, concat_axis=0, tiled=True))

    images, texts = [], []
    for chunk in range(CHUNKS):
        block = arrivals[chunk]
        if slot_total > CAP:
            senders = [jnp.minimum(own_rank + c * member_count, slot_total - 1) for c in range(CAP)]
            block = jnp.stack([lax.dynamic_index_in_dim(block, s, 0, keepdims=False) for s in senders])
        blocks = block.shape[0]
        scaled = layer_norm(block, expert_gain[0]).astype(jnp.bfloat16)
        gathered = lax.all_gather(scaled, "tensor", axis=0).reshape(-1, model_width)
        inner = jax.nn.gelu(matmul(gathered, expert_in[0]), approximate=False).astype(jnp.bfloat16)
        inner = lax.optimization_barrier(inner)
        terms = matmul(inner, expert_out[0]).astype(jnp.bfloat16)
        terms = terms.reshape(tensor_size, blocks * part, model_width)
        done = lax.psum_scatter(terms, "tensor", scatter_dimension=0)
        done = done.reshape(blocks, part, model_width)
        if slot_total > CAP:
            wanted = [jnp.minimum(d // member_count, CAP - 1) for d in range(slot_total)]
            done = jnp.stack([lax.dynamic_index_in_dim(done, w, 0, keepdims=False) for w in wanted])
        returned = lax.all_to_all(done, "dp", split_axis=0, concat_axis=0, tiled=True)
        image_ffn = lax.dynamic_index_in_dim(returned, image_dest, 0, keepdims=False)
        text_ffn = lax.dynamic_index_in_dim(returned, text_dest, 0, keepdims=False)
        hidden = hiddens[chunk].astype(jnp.float32)
        images.append((hidden[0] + image_ffn.astype(jnp.float32)).astype(jnp.bfloat16))
        text_sum = (hidden[1] + text_ffn.astype(jnp.float32)).astype(jnp.bfloat16)
        slot_index = tensor_place * row_count + chunk * part + jnp.arange(part, dtype=jnp.int32)
        live = slot_index[:, None] < text_count[0]
        texts.append(jnp.where(live, text_sum, jnp.zeros_like(text_sum)))
    shape = image_rows.shape
    return (
        jnp.concatenate(images, axis=0).reshape(shape),
        jnp.concatenate(texts, axis=0).reshape(shape),
    )


def solution(mesh):
    return jax.shard_map(
        body,
        mesh=mesh,
        in_specs=(
            P("tensor", "dp", None),
            P("tensor", "dp", None),
            P("dp"),
            P(),
            P(),
            P(None, None, "tensor"),
            P("tensor", None),
            P("dp", None),
            P("dp", None, "tensor"),
            P("dp", "tensor", None),
        ),
        out_specs=(P("tensor", "dp", None), P("tensor", "dp", None)),
        check_vma=False,
    )
```

time: 424 us -> 422 us (level)
  local copies, waits for them, and re-layouts: 27.1 us -> 0.08 us
  blocking collectives: 0 us -> 18.9 us
  waiting for transfers between devices: 233 us -> 250 us
  other arithmetic: 28.3 us -> 12.5 us
    reduce_scatter x2 -> x4, waiting for transfers between devices: 113 us -> 137 us  [the longest x2 76.3 us: body(): attended = lax.psum_scatter(terms, 'tensor', scatter_dimension=0)]
    unnamed x14 -> x12, local copies, waits for them, and re-layouts: 19.4 us -> 0.04 us
    all_to_all x2 -> x3, waiting for transfers between devices: 46.4 us -> 27.6 us  [the longest x2 14.5 us: body(): lax.all_to_all(done, 'dp', split_axis=0, concat_axis=0, tiled=True)]
    all_to_all x0 -> x1, blocking collectives: none -> 18.9 us  [body(): lax.all_to_all(outgoing, 'dp', split_axis=0, concat_axis=0, tiled=True)]
    all_gather x2 -> x4, waiting for transfers between devices: 74.2 us -> 84.1 us  [the longest x2 48.3 us: body(): gathered = lax.all_gather(normed, 'tensor', axis=0).reshape(-1, model_width)]
    select_n x4 -> x3, other arithmetic: 6.66 us -> 1.13 us  [the longest x1 0.96 us: body(): jnp.where((slot_kind == 0)[:, None, None], hidden[0][None], hidden[1][None])]
    reduce_sum x2 -> x3, other arithmetic: 5.9 us -> 1.55 us  [layer_norm(): center = floats - jnp.mean(floats, axis=-1, keepdims=True)]
    all_to_all x2 -> x3, starting transfers between devices: 9.18 us -> 12.7 us  [the longest x2 9.2 us: body(): lax.all_to_all(done, 'dp', split_axis=0, concat_axis=0, tiled=True)]
  transfers between devices with their start and end apart: 6 -> 11, of which waited for: 6 -> 10; matrix products, arithmetic and copies ran while one was open for 6% -> 22% of each run, Pallas kernels for 0% -> 0%
where the time goes in v1:
time: 422 us; the launch traced here: 421 us
  waiting for transfers between devices  250 us (59%)
  matrix products  101 us (24%)
  between operations  21.6 us (5%)
  blocking collectives  18.9 us (4%)
  starting transfers between devices  13.4 us (3%)
  other arithmetic  12.5 us (3%)
    dot_general x12, matrix products, matmul(): return jnp.dot(left, right, preferred_element_type=jnp.float32)  101 us
    reduce_scatter x2, waiting for transfers between devices, body(): attended = lax.psum_scatter(terms, 'tensor', scatter_dimension=0)  76.3 us
    reduce_scatter x2, waiting for transfers between devices, body(): done = lax.psum_scatter(terms, 'tensor', scatter_dimension=0)  60.7 us
    all_gather x2, waiting for transfers between devices, body(): gathered = lax.all_gather(normed, 'tensor', axis=0).reshape(-1, model_width)  48.3 us
    all_gather x2, waiting for transfers between devices, body(): gathered = lax.all_gather(scaled, 'tensor', axis=0).reshape(-1, model_width)  35.8 us
    all_to_all x1, blocking collectives, body(): lax.all_to_all(outgoing, 'dp', split_axis=0, concat_axis=0, tiled=True)  18.9 us
    all_to_all x2, waiting for transfers between devices, body(): lax.all_to_all(done, 'dp', split_axis=0, concat_axis=0, tiled=True)  14.5 us
    all_to_all x1, waiting for transfers between devices, body(): lax.all_to_all(outgoing, 'dp', split_axis=0, concat_axis=0, tiled=True)  13.1 us
  transfers between devices with their start and end apart: 11, of which 10 were waited for; matrix products, arithmetic and copies ran while one was open for 22% of the time, Pallas kernels for 0%

profile of v1, /device:TPU:0, one launch (start us, length us, event | category | flops | bytes accessed | tf_op | source)
XLA Modules:
  0.0 421.2 jit_solution(3676085953000856665)
XLA Ops:
  7.2 1.2 convert_reduce_fusion.3
  8.8 1.7 fusion.89
  12.0 29.3 %all-gather.11.cloned.1.call-done = bf16[16,16,4096]{2,1,0:T(8,128)(2,1)} async-done(((bf16[2,16,4096]{2,1,0:T(8,128)(2,1)}), bf16[16,16,4096]{2,1,0:T(8,128)(2,1)}) %all-gather.11.cloned.1.call-update) | async-done | bytes 2097168 | tf_op jit(solution)/shard_map/all_gather | solution.py:102
  41.3 4.2 fusion.59.q_ref
  45.6 3.5 fusion.65
  49.1 3.6 fusion.71
  52.7 19.0 %all-gather.9.cloned.1.call-done = bf16[16,16,4096]{2,1,0:T(8,128)(2,1)} async-done(((bf16[2,16,4096]{2,1,0:T(8,128)(2,1)}), bf16[16,16,4096]{2,1,0:T(8,128)(2,1)}) %all-gather.9.cloned.1.call-update) | async-done | bytes 2097168 | tf_op jit(solution)/shard_map/all_gather | solution.py:102
  71.7 4.2 fusion.62
  76.0 3.6 fusion.68
  79.7 1.9 shard_map.114
  81.6 2.6 convolution_convert_fusion
  84.2 4.2 fusion.56.q_ref
  88.5 1.9 shard_map.113
  90.4 2.6 convolution_convert_fusion.1
  93.0 32.5 %reduce-scatter.9.cloned.1.call-done = bf16[1,32,4096]{2,1,0:T(8,128)(2,1)} async-done(((bf16[8,32,4096]{2,1,0:T(8,128)(2,1)}), bf16[1,32,4096]{2,1,0:T(8,128)(2,1)}) %reduce-scatter.9.cloned.1.call-update) | async-done | bytes 262160 | tf_op jit(solution)/shard_map/reduce_scatter | solution.py:127
  125.6 1.0 fusion.113
  126.6 43.7 %reduce-scatter.5.cloned.1.call-done = bf16[1,32,4096]{2,1,0:T(8,128)(2,1)} async-done(((bf16[8,32,4096]{2,1,0:T(8,128)(2,1)}), bf16[1,32,4096]{2,1,0:T(8,128)(2,1)}) %reduce-scatter.5.cloned.1.call-update) | async-done | bytes 262160 | tf_op jit(solution)/shard_map/reduce_scatter | solution.py:127
  172.3 18.9 %all_to_all.20 = bf16[4,16,4096]{2,1,0:T(8,128)(2,1)S(1)} all-to-all(bf16[4,16,4096]{2,1,0:T(8,128)(2,1)S(1)} %get-tuple-element.22), channel_id=1, replica_groups=mesh['dp'=4,'tensor'=8] {'dp'}, dimensions={0} | all-to-all | bytes 1048576 | tf_op jit(solution)/shard_map/all_to_all | solution.py:132
  191.2 3.5 all-to-all-start.2
  195.2 13.1 %all-to-all-done.2 = bf16[4,16,4096]{2,1,0:T(8,128)(2,1)S(1)} async-done(((bf16[4,16,4096]{2,1,0:T(8,128)(2,1)}), bf16[4,16,4096]{2,1,0:T(8,128)(2,1)S(1)}, u32[]{:S(2)}, u32[]{:S(2)}) %all-to-all-start.2) | async-done | bytes 524320 | tf_op jit(solution)/shard_map/all_to_all | solution.py:132
  208.8 1.5 fusion.79
  211.1 34.2 %all-gather.15.cloned.1.call-done = bf16[32,16,4096]{2,1,0:T(8,128)(2,1)} async-done(((bf16[4,16,4096]{2,1,0:T(8,128)(2,1)}), bf16[32,16,4096]{2,1,0:T(8,128)(2,1)}) %all-gather.15.cloned.1.call-update) | async-done | bytes 4194320 | tf_op jit(solution)/shard_map/all_gather | solution.py:142
  245.3 22.0 %fusion.19 = bf16[512,2048]{1,0:T(8,128)(2,1)S(1)} fusion(bf16[512,4096]{1,0:T(8,128)(2,1)} %bitcast.115, bf16[1,4096,2048]{2,1,0:T(8,128)(2,1)} %param.18), kind=kOutput, calls=%fused_computation.19 | convolution fusion | flops 8658092032 | bytes 23068672 | tf_op jit(solution)/shard_map/dot_general | solution.py:70
  267.3 14.5 %fusion.11 = bf16[512,4096]{1,0:T(8,128)(2,1)} fusion(bf16[512,2048]{1,0:T(8,128)(2,1)S(1)} %fusion.19, bf16[1,2048,4096]{2,1,0:T(8,128)(2,1)} %param.19), kind=kOutput, calls=%fused_computation.11 | convolution fusion | flops 8592031744 | bytes 23068672 | tf_op jit(solution)/shard_map/dot_general | solution.py:70
  282.1 1.6 all-gather.13.cloned.1.call-done
  283.8 22.1 %fusion.16 = bf16[512,2048]{1,0:T(8,128)(2,1)S(1)} fusion(bf16[512,4096]{1,0:T(8,128)(2,1)} %bitcast.114, bf16[1,4096,2048]{2,1,0:T(8,128)(2,1)} %param.18), kind=kOutput, calls=%fused_computation.16 | convolution fusion | flops 8658092032 | bytes 23068672 | tf_op jit(solution)/shard_map/dot_general | solution.py:70
  305.8 13.9 %fusion.8 = bf16[512,4096]{1,0:T(8,128)(2,1)} fusion(bf16[512,2048]{1,0:T(8,128)(2,1)S(1)} %fusion.16, bf16[1,2048,4096]{2,1,0:T(8,128)(2,1)} %param.19), kind=kOutput, calls=%fused_computation.10 | convolution fusion | flops 8592031744 | bytes 23068672 | tf_op jit(solution)/shard_map/dot_general | solution.py:70
  319.7 18.8 %reduce-scatter.11.cloned.1.call-done = bf16[1,64,4096]{2,1,0:T(8,128)(2,1)} async-done(((bf16[8,64,4096]{2,1,0:T(8,128)(2,1)}), bf16[1,64,4096]{2,1,0:T(8,128)(2,1)}) %reduce-scatter.11.cloned.1.call-update) | async-done | bytes 524304 | tf_op jit(solution)/shard_map/reduce_scatter | solution.py:147
  338.5 4.6 %all-to-all-start.3 = ((bf16[4,16,4096]{2,1,0:T(8,128)(2,1)}), bf16[4,16,4096]{2,1,0:T(8,128)(2,1)S(1)}, u32[]{:S(2)}, u32[]{:S(2)}) async-start(bf16[4,16,4096]{2,1,0:T(8,128)(2,1)} %bitcast.107), calls=%async_computation.7 | async-start | bytes 1048576 | tf_op jit(solution)/shard_map/all_to_all | solution.py:152
  351.7 41.9 %reduce-scatter.7.cloned.1.call-done = bf16[1,64,4096]{2,1,0:T(8,128)(2,1)} async-done(((bf16[8,64,4096]{2,1,0:T(8,128)(2,1)}), bf16[1,64,4096]{2,1,0:T(8,128)(2,1)}) %reduce-scatter.7.cloned.1.call-update) | async-done | bytes 524304 | tf_op jit(solution)/shard_map/reduce_scatter | solution.py:147
  393.6 4.6 %all-to-all-start.1 = ((bf16[4,16,4096]{2,1,0:T(8,128)(2,1)}), bf16[4,16,4096]{2,1,0:T(8,128)(2,1)S(1)}, u32[]{:S(2)}, u32[]{:S(2)}) async-start(bf16[4,16,4096]{2,1,0:T(8,128)(2,1)} %bitcast.108), calls=%async_computation.3 | async-start | bytes 1048576 | tf_op jit(solution)/shard_map/all_to_all | solution.py:152
  398.2 14.5 %all-to-all-done.1 = bf16[4,16,4096]{2,1,0:T(8,128)(2,1)S(1)} async-done(((bf16[4,16,4096]{2,1,0:T(8,128)(2,1)}), bf16[4,16,4096]{2,1,0:T(8,128)(2,1)S(1)}, u32[]{:S(2)}, u32[]{:S(2)}) %all-to-all-start.1) | async-done | bytes 524320 | tf_op jit(solution)/shard_map/all_to_all | solution.py:152
  (61 shorter events, 9.2 us)
Async XLA Ops:
  7.2 34.2 %all-gather.11.cloned.1.call-start = ((), (), s32[]{:S(2)}) async-start(), calls=%async_computation.13 | async-start | bytes 2359296 | tf_op jit(solution)/shard_map/all_gather | solution.py:102
  10.6 61.2 %all-gather.9.cloned.1.call-start = ((), (), s32[]{:S(2)}) async-start(), calls=%async_computation.12 | async-start | bytes 2359296 | tf_op jit(solution)/shard_map/all_gather | solution.py:102
  11.3 114.3 %reduce-scatter.9.cloned.1.call-start = ((), (), s32[]{:S(2)}) async-start(), calls=%async_computation.10 | async-start | bytes 2359296 | tf_op jit(solution)/shard_map/reduce_scatter | solution.py:127
  41.3 4.2 %copy-start.5 = (bf16[16,16,4096]{2,1,0:T(8,128)(2,1)S(1)}, bf16[16,16,4096]{2,1,0:T(8,128)(2,1)}, u32[]{:S(2)}) copy-start(bf16[16,16,4096]{2,1,0:T(8,128)(2,1)} %all-gather.11.cloned.1.call-done) | copy-start | bytes 6291460
  71.7 4.2 %copy-start.4 = (bf16[16,16,4096]{2,1,0:T(8,128)(2,1)S(1)}, bf16[16,16,4096]{2,1,0:T(8,128)(2,1)}, u32[]{:S(2)}) copy-start(bf16[16,16,4096]{2,1,0:T(8,128)(2,1)} %all-gather.9.cloned.1.call-done) | copy-start | bytes 6291460
  76.0 5.6 %copy-start.2 = (bf16[512,4096]{1,0:T(8,128)(2,1)S(1)}, bf16[512,4096]{1,0:T(8,128)(2,1)}, u32[]{:S(2)}) copy-start(bf16[512,4096]{1,0:T(8,128)(2,1)} %param.16) | copy-start | bytes 12582916
  84.2 86.1 %reduce-scatter.5.cloned.1.call-start = ((), (), s32[]{:S(2)}) async-start(), calls=%async_computation.8 | async-start | bytes 2359296 | tf_op jit(solution)/shard_map/reduce_scatter | solution.py:127
  84.2 6.1 %copy-start.3 = (bf16[512,4096]{1,0:T(8,128)(2,1)S(1)}, bf16[512,4096]{1,0:T(8,128)(2,1)}, u32[]{:S(2)}) copy-start(bf16[512,4096]{1,0:T(8,128)(2,1)} %param.16) | copy-start | bytes 12582916
  90.4 2.7 copy-start.1
  126.6 82.2 %copy-start = (f32[1,4096]{1,0:T(1,128)S(1)}, f32[1,4096]{1,0:T(1,128)}, u32[]{:S(2)}) copy-start(f32[1,4096]{1,0:T(1,128)} %param.17) | copy-start | bytes 49156
  191.2 17.1 %all-to-all-start.2 = ((bf16[4,16,4096]{2,1,0:T(8,128)(2,1)}), bf16[4,16,4096]{2,1,0:T(8,128)(2,1)S(1)}, u32[]{:S(2)}, u32[]{:S(2)}) async-start(bf16[4,16,4096]{2,1,0:T(8,128)(2,1)} %get-tuple-element.23), calls=%async_computation.5 | async-start | bytes 1048576 | tf_op jit(solution)/shard_map/all_to_all | solution.py:132
  194.7 50.6 %all-gather.15.cloned.1.call-start = ((), (), s32[]{:S(2)}) async-start(), calls=%async_computation.15 | async-start | bytes 4718592 | tf_op jit(solution)/shard_map/all_gather | solution.py:142
  210.3 73.5 %all-gather.13.cloned.1.call-start = ((), (), s32[]{:S(2)}) async-start(), calls=%async_computation.14 | async-start | bytes 4718592 | tf_op jit(solution)/shard_map/all_gather | solution.py:142
  210.9 127.6 %reduce-scatter.11.cloned.1.call-start = ((), (), s32[]{:S(2)}) async-start(), calls=%async_computation.11 | async-start | bytes 4718592 | tf_op jit(solution)/shard_map/reduce_scatter | solution.py:147
  281.9 111.7 %reduce-scatter.7.cloned.1.call-start = ((), (), s32[]{:S(2)}) async-start(), calls=%async_computation.9 | async-start | bytes 4718592 | tf_op jit(solution)/shard_map/reduce_scatter | solution.py:147
  338.5 55.1 %all-to-all-start.3 = ((bf16[4,16,4096]{2,1,0:T(8,128)(2,1)}), bf16[4,16,4096]{2,1,0:T(8,128)(2,1)S(1)}, u32[]{:S(2)}, u32[]{:S(2)}) async-start(bf16[4,16,4096]{2,1,0:T(8,128)(2,1)} %bitcast.107), calls=%async_computation.7 | async-start | bytes 1048576 | tf_op jit(solution)/shard_map/all_to_all | solution.py:152
  393.6 19.1 %all-to-all-start.1 = ((bf16[4,16,4096]{2,1,0:T(8,128)(2,1)}), bf16[4,16,4096]{2,1,0:T(8,128)(2,1)S(1)}, u32[]{:S(2)}, u32[]{:S(2)}) async-start(bf16[4,16,4096]{2,1,0:T(8,128)(2,1)} %bitcast.108), calls=%async_computation.3 | async-start | bytes 1048576 | tf_op jit(solution)/shard_map/all_to_all | solution.py:152
Sparse Core Ops, SparseCore 0:
  10.7 30.6 all-gather.10
  43.8 27.8 all-gather.8
  84.3 41.2 reduce-scatter.8
  129.1 41.2 reduce-scatter.4
  210.4 34.8 all-gather.14
  247.0 36.7 all-gather.12
  287.1 51.3 reduce-scatter.10
  342.2 51.3 reduce-scatter.6

commit v2 on v1

--- a/solution.py
+++ b/solution.py
@@ -9,7 +9,10 @@
 
 HDIM = 128
 CAP = 4
-CHUNKS = 2
+CHUNKS = 1
+MESH = pl.DeviceIdType.MESH
+TILES = 4
+PIECES = 4
 
 
 def layer_norm(values, gain):
@@ -68,6 +71,229 @@
 
 def matmul(left, right):
     return jnp.dot(left, right, preferred_element_type=jnp.float32)
+
+
+def partners():
+    me = lax.axis_index("tensor")
+    core, across, down = me % 2, me // 2 % 2, me // 4
+    sibling = me + 1 - 2 * core
+    over_x = me + 2 - 4 * across
+    over_y = me + 4 - 8 * down
+    return me, core, across, down, sibling, over_x, over_y
+
+
+def greet(others):
+    barrier = pltpu.get_barrier_semaphore()
+    for other in others:
+        pl.semaphore_signal(barrier, inc=1, device_id={"tensor": other}, device_id_type=MESH)
+    pl.semaphore_wait(barrier, len(others))
+
+
+def remote(source, target, send_sem, recv_sem, other):
+    return pltpu.make_async_remote_copy(
+        src_ref=source,
+        dst_ref=target,
+        send_sem=send_sem,
+        recv_sem=recv_sem,
+        device_id={"tensor": other},
+        device_id_type=MESH,
+    )
+
+
+def gather_kernel(own_ref, all_ref, own_sem, send_sem, recv_sem):
+    me, core, across, down, sibling, over_x, over_y = partners()
+    diagonal = over_x + over_y - me
+    rows = own_ref.shape[0]
+    size = rows // PIECES
+    half = PIECES // 2
+
+    def piece(owner, p):
+        return all_ref.at[owner, pl.ds(p * size, size)]
+
+    greet((sibling, over_x, over_y))
+    sent = []
+
+    def send(source, owner, p, kind, other):
+        copy = remote(source, piece(owner, p), send_sem.at[kind, p], recv_sem.at[kind, p], other)
+        copy.start()
+        sent.append(copy)
+
+    def arrived(owner, p, kind, other):
+        there = piece(owner, p)
+        remote(there, there, send_sem.at[kind, p], recv_sem.at[kind, p], other).wait_recv()
+
+    keep = pltpu.make_async_copy(own_ref, all_ref.at[me], own_sem)
+    for i in range(PIECES):
+        for kind, other, p in ((0, over_x, i), (1, over_y, (i + half) % PIECES)):
+            send(own_ref.at[pl.ds(p * size, size)], me, p, kind, other)
+    for p in range(PIECES):
+        send(own_ref.at[pl.ds(p * size, size)], me, p, 3, sibling)
+    keep.start()
+    for i in range(PIECES):
+        p, q = i, (i + half) % PIECES
+        arrived(over_x, p, 0, over_x)
+        if p < half:
+            send(piece(over_x, p), over_x, p, 2, over_y)
+        send(piece(over_x, p), over_x, p, 4, sibling)
+        arrived(over_y, q, 1, over_y)
+        if q >= half:
+            send(piece(over_y, q), over_y, q, 2, over_x)
+        send(piece(over_y, q), over_y, q, 5, sibling)
+    for i in range(half):
+        for p, other in ((i, over_y), (i + half, over_x)):
+            arrived(diagonal, p, 2, other)
+            send(piece(diagonal, p), diagonal, p, 6, sibling)
+    shift = sibling - me
+    for kind, owner in ((3, sibling), (4, over_x + shift), (5, over_y + shift), (6, diagonal + shift)):
+        for p in range(PIECES):
+            arrived(owner, p, kind, sibling)
+    for copy in sent:
+        copy.wait_send()
+    keep.wait()
+
+
+def gather_rows(values, collective_id):
+    size = lax.axis_size("tensor")
+    if size != 8:
+        return lax.all_gather(values, "tensor", axis=0)
+    return pl.pallas_call(
+        gather_kernel,
+        out_shape=jax.ShapeDtypeStruct((size, *values.shape), values.dtype),
+        in_specs=[pl.BlockSpec(memory_space=pl.ANY)],
+        out_specs=pl.BlockSpec(memory_space=pl.ANY),
+        scratch_shapes=[
+            pltpu.SemaphoreType.DMA,
+            pltpu.SemaphoreType.DMA((7, PIECES)),
+            pltpu.SemaphoreType.DMA((7, PIECES)),
+        ],
+        compiler_params=pltpu.CompilerParams(collective_id=collective_id, has_side_effects=True),
+    )(values)
+
+
+def scatter_kernel(
+    left_ref, weight_ref, out_ref, weight, terms, first, second, third, w_sem, send_sem, recv_sem
+):
+    me, core, across, down, sibling, over_x, over_y = partners()
+    n = left_ref.shape[1]
+    half = n // 2
+    depth = left_ref.shape[2]
+    wide = weight.shape[2]
+    step = 512
+    loads = [
+        pltpu.make_async_copy(
+            weight_ref.at[:, pl.ds(j * wide, wide)], weight.at[j], w_sem.at[j]
+        )
+        for j in range(TILES)
+    ]
+    for load in loads:
+        load.start()
+    greet((sibling, over_x, over_y))
+    sent = []
+
+    def send(source, target, kind, j, other):
+        copy = remote(source, target, send_sem.at[kind, j], recv_sem.at[kind, j], other)
+        copy.start()
+        sent.append(copy)
+
+    def arrived(there, kind, j, other):
+        remote(there, there, send_sem.at[kind, j], recv_sem.at[kind, j], other).wait_recv()
+
+    low, high = pl.ds(0, half), pl.ds(half, half)
+    here = 2 * down + across
+    beside_x, beside_y = 2 * down + 1 - across, 2 * (1 - down) + across
+    opposite = 3 - here
+
+    def add(*refs):
+        total = refs[0][...].astype(jnp.float32)
+        for ref in refs[1:]:
+            total = total + ref[...].astype(jnp.float32)
+        return total
+
+    def multiply(j):
+        loads[j].wait()
+
+        @pl.loop(0, 4)
+        def _(chip):
+            rows = left_ref[pl.ds(2 * chip, 2)].reshape(2 * n, depth)
+            for c in range(wide // step):
+                columns = slice(c * step, (c + 1) * step)
+                product = jnp.dot(rows, weight[j, :, columns], preferred_element_type=jnp.float32)
+                product = product.astype(terms.dtype).reshape(2, n, step)
+                terms[j, 0, chip, :, columns] = product[0]
+                terms[j, 1, chip, :, columns] = product[1]
+
+        send(terms.at[j, 1 - core], first.at[j], 0, j, sibling)
+
+    def stage_two(j):
+        arrived(first.at[j], 0, j, sibling)
+
+        @pl.loop(0, 4)
+        def _(chip):
+            first[j, chip] = add(terms.at[j, core, chip], first.at[j, chip]).astype(first.dtype)
+
+        send(first.at[j, opposite, low], second.at[j, 1, low], 1, j, over_x)
+        send(first.at[j, opposite, high], second.at[j, 1, high], 2, j, over_y)
+        send(first.at[j, beside_x, low], second.at[j, 0, low], 3, j, over_x)
+        send(first.at[j, beside_y, high], second.at[j, 0, high], 4, j, over_y)
+
+    def stage_three(j):
+        arrived(second.at[j, 1, low], 1, j, over_x)
+        arrived(second.at[j, 1, high], 2, j, over_y)
+        second[j, 1, low] = add(first.at[j, beside_y, low], second.at[j, 1, low]).astype(second.dtype)
+        second[j, 1, high] = add(first.at[j, beside_x, high], second.at[j, 1, high]).astype(second.dtype)
+        send(second.at[j, 1, low], third.at[j, low], 5, j, over_y)
+        send(second.at[j, 1, high], third.at[j, high], 6, j, over_x)
+
+    def finish(j):
+        arrived(second.at[j, 0, low], 3, j, over_x)
+        arrived(second.at[j, 0, high], 4, j, over_y)
+        arrived(third.at[j, low], 5, j, over_y)
+        arrived(third.at[j, high], 6, j, over_x)
+        total = add(first.at[j, here], second.at[j, 0], third.at[j])
+        out_ref[:, j * wide : (j + 1) * wide] = total.astype(out_ref.dtype)
+
+    for j in range(TILES + 3):
+        if j < TILES:
+            multiply(j)
+        if 1 <= j <= TILES:
+            stage_two(j - 1)
+        if 2 <= j <= TILES + 1:
+            stage_three(j - 2)
+        if j >= 3:
+            finish(j - 3)
+    for copy in sent:
+        copy.wait_send()
+
+
+def multiply_scatter(left, weight, dtype, collective_id):
+    size, n, depth = left.shape
+    width = weight.shape[1]
+    if size != 8:
+        terms = matmul(left.reshape(size * n, depth), weight).astype(jnp.bfloat16)
+        return lax.psum_scatter(terms.reshape(size, n, width), "tensor", scatter_dimension=0).astype(dtype)
+    wide = width // TILES
+    return pl.pallas_call(
+        scatter_kernel,
+        out_shape=jax.ShapeDtypeStruct((n, width), dtype),
+        in_specs=[pl.BlockSpec(memory_space=pltpu.VMEM), pl.BlockSpec(memory_space=pl.ANY)],
+        out_specs=pl.BlockSpec(memory_space=pltpu.VMEM),
+        scratch_shapes=[
+            pltpu.VMEM((TILES, depth, wide), jnp.bfloat16),
+            pltpu.VMEM((TILES, 2, 4, n, wide), jnp.bfloat16),
+            pltpu.VMEM((TILES, 4, n, wide), jnp.bfloat16),
+            pltpu.VMEM((TILES, 2, n, wide), jnp.bfloat16),
+            pltpu.VMEM((TILES, n, wide), jnp.bfloat16),
+            pltpu.SemaphoreType.DMA((TILES,)),
+            pltpu.SemaphoreType.DMA((7, TILES)),
+            pltpu.SemaphoreType.DMA((7, TILES)),
+        ],
+        compiler_params=pltpu.CompilerParams(
+            collective_id=collective_id, has_side_effects=True, vmem_limit_bytes=52 * 2**20
+        ),
+        cost_estimate=pl.CostEstimate(
+            flops=2 * size * n * depth * width, bytes_accessed=2 * depth * width, transcendentals=0
+        ),
+    )(left, weight)
 
 
 def body(
@@ -99,7 +325,7 @@
     projected = []
     for chunk in range(CHUNKS):
         normed = layer_norm(rows_of(chunk), attn_gain).astype(jnp.bfloat16)
-        gathered = lax.all_gather(normed, "tensor", axis=0).reshape(-1, model_width)
+        gathered = gather_rows(normed.reshape(2 * part, model_width), 0).reshape(-1, model_width)
         projected.append(
             [matmul(gathered, qkv_weight[:, i]).astype(jnp.bfloat16) for i in range(3)]
         )
@@ -122,10 +348,10 @@
     hiddens, arrivals = [], []
     for chunk in range(CHUNKS):
         context = attention(live_keys, projected[chunk][0], keys, values)
-        terms = matmul(context, out_weight).astype(jnp.bfloat16)
-        terms = terms.reshape(tensor_size, 2 * part, model_width)
-        attended = lax.psum_scatter(terms, "tensor", scatter_dimension=0)
-        attended = attended.reshape(2, part, model_width).astype(jnp.float32)
+        attended = multiply_scatter(
+            context.reshape(tensor_size, 2 * part, -1), out_weight, jnp.float32, 2
+        )
+        attended = attended.reshape(2, part, model_width)
         hidden = (rows_of(chunk).astype(jnp.float32) + attended).astype(jnp.bfloat16)
         hiddens.append(hidden)
         outgoing = jnp.where((slot_kind == 0)[:, None, None], hidden[0][None], hidden[1][None])
@@ -139,12 +365,11 @@
             block = jnp.stack([lax.dynamic_index_in_dim(block, s, 0, keepdims=False) for s in senders])
         blocks = block.shape[0]
         scaled = layer_norm(block, expert_gain[0]).astype(jnp.bfloat16)
-        gathered = lax.all_gather(scaled, "tensor", axis=0).reshape(-1, model_width)
+        gathered = gather_rows(scaled.reshape(blocks * part, model_width), 1).reshape(-1, model_width)
         inner = jax.nn.gelu(matmul(gathered, expert_in[0]), approximate=False).astype(jnp.bfloat16)
-        inner = lax.optimization_barrier(inner)
-        terms = matmul(inner, expert_out[0]).astype(jnp.bfloat16)
-        terms = terms.reshape(tensor_size, blocks * part, model_width)
-        done = lax.psum_scatter(terms, "tensor", scatter_dimension=0)
+        done = multiply_scatter(
+            inner.reshape(tensor_size, blocks * part, -1), expert_out[0], jnp.bfloat16, 3
+        )
         done = done.reshape(blocks, part, model_width)
         if slot_total > CAP:
             wanted = [jnp.minimum(d // member_count, CAP - 1) for d in range(slot_total)]

time: 422 us -> 267 us (0.63)
  waiting for transfers between devices: 250 us -> 17 us
  Pallas kernels: 3.75 us -> 141 us
  matrix products: 101 us -> 55.5 us
  between operations: 21.6 us -> 8.28 us
  blocking collectives: 18.9 us -> 30.1 us
  starting transfers between devices: 13.4 us -> 3.53 us
    pallas_call x0 -> x4, Pallas kernels: none -> 139 us  [the longest x2 76 us: multiply_scatter(): pl.pallas_call(scatter_kernel, out_shape=jax.ShapeDtypeStruct((n, width),...]
    reduce_scatter x4 -> x0, waiting for transfers between devices: 137 us -> none  [the longest x2 76.3 us: body(): attended = lax.psum_scatter(terms, 'tensor', scatter_dimension=0)]
    all_gather x4 -> x0, waiting for transfers between devices: 84.1 us -> none  [the longest x2 48.3 us: body(): gathered = lax.all_gather(normed, 'tensor', axis=0).reshape(-1, model_width)]
    dot_general x12 -> x4, matrix products: 101 us -> 55.5 us  [matmul(): return jnp.dot(left, right, preferred_element_type=jnp.float32)]
    all_to_all x1 -> x0, waiting for transfers between devices: 13.1 us -> none  [body(): lax.all_to_all(outgoing, 'dp', split_axis=0, concat_axis=0, tiled=True)]
    all_to_all x1, blocking collectives: 18.9 us -> 30.1 us  [body(): lax.all_to_all(outgoing, 'dp', split_axis=0, concat_axis=0, tiled=True)]
    all_to_all x2 -> x1, starting transfers between devices: 9.2 us -> 3.53 us  [body(): lax.all_to_all(done, 'dp', split_axis=0, concat_axis=0, tiled=True)]
    all_to_all x2 -> x1, waiting for transfers between devices: 14.5 us -> 17 us  [body(): lax.all_to_all(done, 'dp', split_axis=0, concat_axis=0, tiled=True)]
  transfers between devices with their start and end apart: 11 -> 1, of which waited for: 10 -> 1; matrix products, arithmetic and copies ran while one was open for 22% -> 1% of each run, Pallas kernels for 0% -> 0%
where the time goes in v2:
time: 267 us
  Pallas kernels  141 us (53%)
  matrix products  55.5 us (21%)
  blocking collectives  30.1 us (11%)
  waiting for transfers between devices  17 us (6%)
  other arithmetic  10.9 us (4%)
  between operations  8.28 us (3%)
  starting transfers between devices  3.53 us (1%)
    pallas_call x2, Pallas kernels, multiply_scatter(): pl.pallas_call(scatter_kernel, out_shape=jax.ShapeDtypeStruct((n, width),...  76 us
    pallas_call x2, Pallas kernels, gather_rows(): pl.pallas_call(gather_kernel, out_shape=jax.ShapeDtypeStruct((size, *valu...  62.9 us
    dot_general x4, matrix products, matmul(): return jnp.dot(left, right, preferred_element_type=jnp.float32)  55.5 us
    all_to_all x1, blocking collectives, body(): lax.all_to_all(outgoing, 'dp', split_axis=0, concat_axis=0, tiled=True)  30.1 us
    all_to_all x1, waiting for transfers between devices, body(): lax.all_to_all(done, 'dp', split_axis=0, concat_axis=0, tiled=True)  17 us
  transfers between devices with their start and end apart: 1, of which 1 were waited for; matrix products, arithmetic and copies ran while one was open for 1% of the time, Pallas kernels for 0%

profile of v2, /device:TPU:0, one launch (start us, length us, event | category | flops | bytes accessed | tf_op | source)
XLA Modules:
  0.0 266.6 jit_solution(7112799945295526663)
XLA Ops:
  0.6 1.2 convert_reduce_fusion.1
  1.8 0.1 div.53
  1.9 1.3 multiply_reduce_fusion
  3.3 0.1 rsqrt.20
  3.3 2.1 fusion.37.own_ref
  5.4 24.0 %shard_map.113 = bf16[8,64,4096]{2,1,0:T(8,128)(2,1)} custom-call(bf16[64,4096]{1,0:T(8,128)(2,1)} %fusion.37.own_ref), custom_call_target="tpu_custom_call" | custom-call | tf_op jit(solution)/shard_map/pallas_call | solution.py:159
  29.5 5.9 %fusion.32.v_ref = bf16[512,512]{1,0:T(8,128)(2,1)S(1)} fusion(bf16[512,4096]{1,0:T(8,128)(2,1)} %bitcast.68, bf16[4096,3,512]{2,0,1:T(8,128)(2,1)} %param.15), kind=kOutput, calls=%fused_computation.39 | convolution fusion | flops 2147745792 | bytes 8912896 | tf_op jit(solution)/shard_map/dot_general | solution.py:73
  35.4 4.6 %fusion.29.k_ref = bf16[512,512]{1,0:T(8,128)(2,1)S(1)} fusion(bf16[512,4096]{1,0:T(8,128)(2,1)S(1)} %bitcast.69, bf16[4096,3,512]{2,0,1:T(8,128)(2,1)} %param.15), kind=kOutput, calls=%fused_computation.38 | convolution fusion | flops 2147745792 | bytes 8912896 | tf_op jit(solution)/shard_map/dot_general | solution.py:73
  40.0 0.0 copy-start.4
  40.0 4.6 %fusion.26.q_ref = bf16[512,512]{1,0:T(8,128)(2,1)S(1)} fusion(bf16[512,4096]{1,0:T(8,128)(2,1)S(1)} %bitcast.70, bf16[4096,3,512]{2,0,1:T(8,128)(2,1)} %param.15), kind=kOutput, calls=%fused_computation.37 | convolution fusion | flops 2147745792 | bytes 8912896 | tf_op jit(solution)/shard_map/dot_general | solution.py:73
  44.5 0.0 copy-start
  44.5 0.0 copy-start.1
  45.3 2.2 shard_map.114
  47.5 0.0 copy-start.3
  47.5 23.8 %shard_map.115 = f32[64,4096]{1,0:T(8,128)S(1)} custom-call(bf16[8,64,512]{2,1,0:T(8,128)(2,1)S(1)} %bitcast.57, bf16[512,4096]{1,0:T(8,128)(2,1)} %weight_ref.1), custom_call_target="tpu_custom_call" | custom-call | flops 2147483648 | bytes 4194304 | tf_op jit(solution)/shard_map/pallas_call | solution.py:275
  71.3 0.1 fusion.50
  71.5 0.2 broadcast_select_fusion
  71.7 30.1 %all_to_all.10 = bf16[4,32,4096]{2,1,0:T(8,128)(2,1)S(1)} all-to-all(bf16[4,32,4096]{2,1,0:T(8,128)(2,1)S(1)} %broadcast_select_fusion), channel_id=1, replica_groups=mesh['dp'=4,'tensor'=8] {'dp'}, dimensions={0} | all-to-all | bytes 2097152 | tf_op jit(solution)/shard_map/all_to_all | solution.py:358
  101.8 0.2 convert_reduce_fusion
  102.1 0.4 fusion.23
  102.5 1.5 fusion.25
  104.0 38.8 %shard_map.116 = bf16[8,128,4096]{2,1,0:T(8,128)(2,1)} custom-call(bf16[128,4096]{1,0:T(8,128)(2,1)} %bitcast.59), custom_call_target="tpu_custom_call" | custom-call | tf_op jit(solution)/shard_map/pallas_call | solution.py:159
  142.9 40.4 %fusion.4 = bf16[1024,2048]{1,0:T(8,128)(2,1)} fusion(bf16[1024,4096]{1,0:T(8,128)(2,1)} %bitcast.58, bf16[1,4096,2048]{2,1,0:T(8,128)(2,1)} %param.18), kind=kOutput, calls=%fused_computation.5 | convolution fusion | flops 17316184064 | bytes 29360128 | tf_op jit(solution)/shard_map/dot_general | solution.py:73
  183.3 52.2 %shard_map.117 = bf16[128,4096]{1,0:T(8,128)(2,1)} custom-call(bf16[8,128,2048]{2,1,0:T(8,128)(2,1)} %bitcast.73, bf16[2048,4096]{1,0:T(8,128)(2,1)} %bitcast.72), custom_call_target="tpu_custom_call" | custom-call | flops 17179869184 | bytes 16777216 | tf_op jit(solution)/shard_map/pallas_call | solution.py:275
  235.6 3.5 %all-to-all-start.1 = ((bf16[4,32,4096]{2,1,0:T(8,128)(2,1)}), bf16[4,32,4096]{2,1,0:T(8,128)(2,1)S(1)}, u32[]{:S(2)}, u32[]{:S(2)}) async-start(bf16[4,32,4096]{2,1,0:T(8,128)(2,1)} %bitcast.18), calls=%async_computation.1 | async-start | bytes 2097152 | tf_op jit(solution)/shard_map/all_to_all | solution.py:377
  239.1 0.6 fusion.48
  241.0 0.1 select_reduce_fusion
  241.2 0.7 fusion.47
  243.3 0.7 fusion.46
  248.1 17.0 %all-to-all-done.1 = bf16[4,32,4096]{2,1,0:T(8,128)(2,1)S(1)} async-done(((bf16[4,32,4096]{2,1,0:T(8,128)(2,1)}), bf16[4,32,4096]{2,1,0:T(8,128)(2,1)S(1)}, u32[]{:S(2)}, u32[]{:S(2)}) %all-to-all-start.1) | async-done | bytes 1048608 | tf_op jit(solution)/shard_map/all_to_all | solution.py:377
  265.1 0.8 fusion.40
  265.8 0.8 fusion.42
  (14 shorter events, 0.1 us)
Async XLA Ops:
  29.5 5.9 %copy-start.2 = (bf16[8,64,4096]{2,1,0:T(8,128)(2,1)S(1)}, bf16[8,64,4096]{2,1,0:T(8,128)(2,1)}, u32[]{:S(2)}) copy-start(bf16[8,64,4096]{2,1,0:T(8,128)(2,1)} %shard_map.113) | copy-start | bytes 12582916
  40.0 5.3 %copy-start.4 = (s32[4]{0:T(128)S(1)}, s32[4]{0:T(128)}, u32[]{:S(2)}) copy-start(s32[4]{0:T(128)} %param.13) | copy-start | bytes 52
  44.5 26.8 %copy-start = (bf16[32,1,4096]{2,0,1:T(8,128)(2,1)S(1)}, bf16[32,1,4096]{2,0,1:T(8,128)(2,1)}, u32[]{:S(2)}) copy-start(bf16[32,1,4096]{2,0,1:T(8,128)(2,1)} %param.11) | copy-start | bytes 786436
  44.5 26.8 %copy-start.1 = (bf16[32,1,4096]{2,0,1:T(8,128)(2,1)S(1)}, bf16[32,1,4096]{2,0,1:T(8,128)(2,1)}, u32[]{:S(2)}) copy-start(bf16[32,1,4096]{2,0,1:T(8,128)(2,1)} %param.10) | copy-start | bytes 786436
  47.5 55.0 %copy-start.3 = (f32[1,4096]{1,0:T(1,128)S(1)}, f32[1,4096]{1,0:T(1,128)}, u32[]{:S(2)}) copy-start(f32[1,4096]{1,0:T(1,128)} %param.17) | copy-start | bytes 49156
  235.6 29.5 %all-to-all-start.1 = ((bf16[4,32,4096]{2,1,0:T(8,128)(2,1)}), bf16[4,32,4096]{2,1,0:T(8,128)(2,1)S(1)}, u32[]{:S(2)}, u32[]{:S(2)}) async-start(bf16[4,32,4096]{2,1,0:T(8,128)(2,1)} %bitcast.18), calls=%async_computation.1 | async-start | bytes 2097152 | tf_op jit(solution)/shard_map/all_to_all | solution.py:377

commit v3 on v2

--- a/solution.py
+++ b/solution.py
@@ -100,12 +100,27 @@
     )
 
 
-def gather_kernel(own_ref, all_ref, own_sem, send_sem, recv_sem):
+def gather_kernel(
+    gelu, own_ref, weight_ref, out_ref, weight, all_ref, own_sem, w_sem, send_sem, recv_sem
+):
     me, core, across, down, sibling, over_x, over_y = partners()
     diagonal = over_x + over_y - me
+    shift = sibling - me
     rows = own_ref.shape[0]
     size = rows // PIECES
     half = PIECES // 2
+    tiles, _, wide = weight.shape
+    per = weight_ref.shape[2] // wide
+    loads = [
+        pltpu.make_async_copy(
+            weight_ref.at[j // per, :, pl.ds(j % per * wide, wide)], weight.at[j], w_sem.at[j]
+        )
+        for j in range(tiles)
+    ]
+    for load in loads:
+        load.start()
+    keep = pltpu.make_async_copy(own_ref, all_ref.at[me], own_sem)
+    keep.start()
 
     def piece(owner, p):
         return all_ref.at[owner, pl.ds(p * size, size)]
@@ -122,52 +137,102 @@
         there = piece(owner, p)
         remote(there, there, send_sem.at[kind, p], recv_sem.at[kind, p], other).wait_recv()
 
-    keep = pltpu.make_async_copy(own_ref, all_ref.at[me], own_sem)
+    def multiply(blocks):
+        @pl.loop(0, tiles)
+        def _(j):
+            left = jnp.concatenate([all_ref[o, pl.ds(r, c)] for o, r, c in blocks], axis=0)
+            product = jnp.dot(left, weight[j], preferred_element_type=jnp.float32)
+            if gelu:
+                product = 0.5 * product * (1.0 + lax.erf(product * 0.5**0.5))
+            product = product.astype(out_ref.dtype)
+            columns = pl.ds(pl.multiple_of(j * wide, wide), wide)
+            start = 0
+            for o, r, c in blocks:
+                out_ref[o, pl.ds(r, c), columns] = product[start : start + c]
+                start += c
+
     for i in range(PIECES):
         for kind, other, p in ((0, over_x, i), (1, over_y, (i + half) % PIECES)):
             send(own_ref.at[pl.ds(p * size, size)], me, p, kind, other)
     for p in range(PIECES):
         send(own_ref.at[pl.ds(p * size, size)], me, p, 3, sibling)
-    keep.start()
-    for i in range(PIECES):
+    for load in loads:
+        load.wait()
+    keep.wait()
+    for p in range(PIECES):
+        arrived(sibling, p, 3, sibling)
+    multiply([(me, 0, rows), (sibling, 0, rows)])
+
+    def pass_on(i):
         p, q = i, (i + half) % PIECES
         arrived(over_x, p, 0, over_x)
         if p < half:
             send(piece(over_x, p), over_x, p, 2, over_y)
-        send(piece(over_x, p), over_x, p, 4, sibling)
         arrived(over_y, q, 1, over_y)
         if q >= half:
             send(piece(over_y, q), over_y, q, 2, over_x)
+        send(piece(over_x, p), over_x, p, 4, sibling)
         send(piece(over_y, q), over_y, q, 5, sibling)
+
+    def neighbours(first):
+        for i in range(first, first + half):
+            arrived(over_x + shift, i, 4, sibling)
+            arrived(over_y + shift, (i + half) % PIECES, 5, sibling)
+        low, high = first * size, (first + half) % PIECES * size
+        multiply(
+            [(o, r, half * size) for o, r in (
+                (over_x, low), (over_x + shift, low), (over_y, high), (over_y + shift, high)
+            )]
+        )
+
+    for i in range(half):
+        pass_on(i)
+    neighbours(0)
+    for i in range(half, PIECES):
+        pass_on(i)
+    neighbours(half)
     for i in range(half):
         for p, other in ((i, over_y), (i + half, over_x)):
             arrived(diagonal, p, 2, other)
             send(piece(diagonal, p), diagonal, p, 6, sibling)
-    shift = sibling - me
-    for kind, owner in ((3, sibling), (4, over_x + shift), (5, over_y + shift), (6, diagonal + shift)):
-        for p in range(PIECES):
-            arrived(owner, p, kind, sibling)
+    for p in range(PIECES):
+        arrived(diagonal + shift, p, 6, sibling)
+    multiply([(diagonal, 0, rows), (diagonal + shift, 0, rows)])
     for copy in sent:
         copy.wait_send()
-    keep.wait()
-
-
-def gather_rows(values, collective_id):
+
+
+def gather_multiply(values, weight, gelu, collective_id):
     size = lax.axis_size("tensor")
+    n, depth = values.shape
+    width = weight.shape[0] * weight.shape[2]
     if size != 8:
-        return lax.all_gather(values, "tensor", axis=0)
+        gathered = lax.all_gather(values, "tensor", axis=0).reshape(size * n, depth)
+        product = jnp.concatenate([matmul(gathered, w) for w in weight], axis=1)
+        if gelu:
+            product = jax.nn.gelu(product, approximate=False)
+        return product.astype(jnp.bfloat16).reshape(size, n, width)
+    wide = 256
     return pl.pallas_call(
-        gather_kernel,
-        out_shape=jax.ShapeDtypeStruct((size, *values.shape), values.dtype),
-        in_specs=[pl.BlockSpec(memory_space=pl.ANY)],
-        out_specs=pl.BlockSpec(memory_space=pl.ANY),
+        functools.partial(gather_kernel, gelu),
+        out_shape=jax.ShapeDtypeStruct((size, n, width), values.dtype),
+        in_specs=[pl.BlockSpec(memory_space=pltpu.VMEM), pl.BlockSpec(memory_space=pl.ANY)],
+        out_specs=pl.BlockSpec(memory_space=pltpu.VMEM),
         scratch_shapes=[
+            pltpu.VMEM((width // wide, depth, wide), jnp.bfloat16),
+            pltpu.VMEM((size, n, depth), jnp.bfloat16),
             pltpu.SemaphoreType.DMA,
+            pltpu.SemaphoreType.DMA((width // wide,)),
             pltpu.SemaphoreType.DMA((7, PIECES)),
             pltpu.SemaphoreType.DMA((7, PIECES)),
         ],
-        compiler_params=pltpu.CompilerParams(collective_id=collective_id, has_side_effects=True),
-    )(values)
+        compiler_params=pltpu.CompilerParams(
+            collective_id=collective_id, has_side_effects=True, vmem_limit_bytes=52 * 2**20
+        ),
+        cost_estimate=pl.CostEstimate(
+            flops=2 * size * n * depth * width, bytes_accessed=2 * depth * width, transcendentals=0
+        ),
+    )(values, weight)
 
 
 def scatter_kernel(
@@ -325,10 +390,10 @@
     projected = []
     for chunk in range(CHUNKS):
         normed = layer_norm(rows_of(chunk), attn_gain).astype(jnp.bfloat16)
-        gathered = gather_rows(normed.reshape(2 * part, model_width), 0).reshape(-1, model_width)
-        projected.append(
-            [matmul(gathered, qkv_weight[:, i]).astype(jnp.bfloat16) for i in range(3)]
-        )
+        mixed = gather_multiply(
+            normed.reshape(2 * part, model_width), jnp.transpose(qkv_weight, (1, 0, 2)), False, 0
+        )
+        projected.append(jnp.split(mixed.reshape(tensor_size * 2 * part, -1), 3, axis=1))
     keys = jnp.concatenate([p[1] for p in projected], axis=0)
     values = jnp.concatenate([p[2] for p in projected], axis=0)
     place = jnp.arange(CHUNKS * tensor_size * 2 * part, dtype=jnp.int32)
@@ -365,10 +430,11 @@
             block = jnp.stack([lax.dynamic_index_in_dim(block, s, 0, keepdims=False) for s in senders])
         blocks = block.shape[0]
         scaled = layer_norm(block, expert_gain[0]).astype(jnp.bfloat16)
-        gathered = gather_rows(scaled.reshape(blocks * part, model_width), 1).reshape(-1, model_width)
-        inner = jax.nn.gelu(matmul(gathered, expert_in[0]), approximate=False).astype(jnp.bfloat16)
+        inner = gather_multiply(
+            scaled.reshape(blocks * part, model_width), expert_in, True, 1
+        )
         done = multiply_scatter(
-            inner.reshape(tensor_size, blocks * part, -1), expert_out[0], jnp.bfloat16, 3
+            inner, expert_out[0], jnp.bfloat16, 3
         )
         done = done.reshape(blocks, part, model_width)
         if slot_total > CAP:

time: 267 us -> 221 us (0.83)
  matrix products: 55.5 us -> 0 us
  Pallas kernels: 141 us -> 150 us
    dot_general x4 -> x0, matrix products: 55.5 us -> none  [matmul(): return jnp.dot(left, right, preferred_element_type=jnp.float32)]
    pallas_call x2, Pallas kernels: 62.9 us -> 72.9 us  [gather_multiply(): pl.pallas_call(functools.partial(gather_kernel, gelu), out_shape=jax.Shap...]
where the time goes in v3:
time: 221 us
  Pallas kernels  150 us (68%)
  blocking collectives  30.3 us (14%)
  waiting for transfers between devices  17.7 us (8%)
  other arithmetic  9.67 us (4%)
  between operations  8.2 us (4%)
  starting transfers between devices  3.53 us (2%)
    pallas_call x2, Pallas kernels, multiply_scatter(): pl.pallas_call(scatter_kernel, out_shape=jax.ShapeDtypeStruct((n, width),...  74.8 us
    pallas_call x2, Pallas kernels, gather_multiply(): pl.pallas_call(functools.partial(gather_kernel, gelu), out_shape=jax.Shap...  72.9 us
    all_to_all x1, blocking collectives, body(): lax.all_to_all(outgoing, 'dp', split_axis=0, concat_axis=0, tiled=True)  30.3 us
    all_to_all x1, waiting for transfers between devices, body(): lax.all_to_all(done, 'dp', split_axis=0, concat_axis=0, tiled=True)  17.7 us
  transfers between devices with their start and end apart: 1, of which 1 were waited for; matrix products, arithmetic and copies ran while one was open for 1% of the time, Pallas kernels for 0%

profile of v3, /device:TPU:0, one launch (start us, length us, event | category | flops | bytes accessed | tf_op | source)
XLA Modules:
  0.0 220.9 jit_solution(15078388660564812556)
XLA Ops:
  0.6 1.2 convert_reduce_fusion.1
  1.8 0.1 div.53
  1.9 1.3 multiply_reduce_fusion
  3.9 0.1 rsqrt.20
  4.0 0.7 compare_convert_fusion
  4.7 1.3 fusion.7.own_ref
  5.9 27.5 %shard_map.113 = bf16[8,64,1536]{2,1,0:T(8,128)(2,1)} custom-call(bf16[64,4096]{1,0:T(8,128)(2,1)S(1)} %fusion.7.own_ref, bf16[3,4096,512]{2,1,0:T(8,128)(2,1)} %bitcast.45), custom_call_target="tpu_custom_call" | custom-call | flops 6442450944 | bytes 12582912 | tf_op jit(solution)/shard_map/pallas_call | solution.py:216
  33.4 1.5 fusion.21
  34.9 2.2 shard_map.114
  37.1 0.0 copy-start
  37.1 0.0 copy-start.1
  37.1 23.7 %shard_map.115 = f32[64,4096]{1,0:T(8,128)S(1)} custom-call(bf16[8,64,512]{2,1,0:T(8,128)(2,1)S(1)} %bitcast.33, bf16[512,4096]{1,0:T(8,128)(2,1)} %weight_ref.2), custom_call_target="tpu_custom_call" | custom-call | flops 2147483648 | bytes 4194304 | tf_op jit(solution)/shard_map/pallas_call | solution.py:340
  60.8 0.0 copy-done
  60.8 0.1 fusion.20
  61.0 0.2 broadcast_select_fusion
  61.2 0.0 copy-start.2
  61.2 30.3 %all_to_all.10 = bf16[4,32,4096]{2,1,0:T(8,128)(2,1)S(1)} all-to-all(bf16[4,32,4096]{2,1,0:T(8,128)(2,1)S(1)} %broadcast_select_fusion), channel_id=1, replica_groups=mesh['dp'=4,'tensor'=8] {'dp'}, dimensions={0} | all-to-all | bytes 2097152 | tf_op jit(solution)/shard_map/all_to_all | solution.py:423
  91.5 0.2 convert_reduce_fusion
  91.7 0.4 fusion.2
  92.2 0.4 fusion.4
  92.6 45.4 %shard_map.116.left_ref = bf16[8,128,2048]{2,1,0:T(8,128)(2,1)} custom-call(bf16[128,4096]{1,0:T(8,128)(2,1)S(1)} %bitcast.32, bf16[1,4096,2048]{2,1,0:T(8,128)(2,1)} %weight_ref.3), custom_call_target="tpu_custom_call" | custom-call | flops 17179869184 | bytes 16777216 | tf_op jit(solution)/shard_map/pallas_call | solution.py:216
  138.1 51.1 %shard_map.117 = bf16[128,4096]{1,0:T(8,128)(2,1)} custom-call(bf16[8,128,2048]{2,1,0:T(8,128)(2,1)} %shard_map.116.left_ref, bf16[2048,4096]{1,0:T(8,128)(2,1)} %bitcast.44), custom_call_target="tpu_custom_call" | custom-call | flops 17179869184 | bytes 16777216 | tf_op jit(solution)/shard_map/pallas_call | solution.py:340
  189.1 0.0 copy-start.3
  189.1 3.5 %all-to-all-start.1 = ((bf16[4,32,4096]{2,1,0:T(8,128)(2,1)}), bf16[4,32,4096]{2,1,0:T(8,128)(2,1)S(1)}, u32[]{:S(2)}, u32[]{:S(2)}) async-start(bf16[4,32,4096]{2,1,0:T(8,128)(2,1)} %bitcast.13), calls=%async_computation.1 | async-start | bytes 2097152 | tf_op jit(solution)/shard_map/all_to_all | solution.py:443
  192.7 0.0 copy-done.3
  192.7 0.6 fusion.18
  194.6 0.1 select_reduce_fusion
  194.8 0.7 fusion.17
  196.9 0.7 fusion.16
  201.7 17.7 %all-to-all-done.1 = bf16[4,32,4096]{2,1,0:T(8,128)(2,1)S(1)} async-done(((bf16[4,32,4096]{2,1,0:T(8,128)(2,1)}), bf16[4,32,4096]{2,1,0:T(8,128)(2,1)S(1)}, u32[]{:S(2)}, u32[]{:S(2)}) %all-to-all-start.1) | async-done | bytes 1048608 | tf_op jit(solution)/shard_map/all_to_all | solution.py:443
  219.3 0.8 fusion.10
  220.1 0.8 fusion.12
  (9 shorter events, 0.1 us)
Async XLA Ops:
  37.1 23.8 %copy-start = (bf16[32,1,4096]{2,0,1:T(8,128)(2,1)S(1)}, bf16[32,1,4096]{2,0,1:T(8,128)(2,1)}, u32[]{:S(2)}) copy-start(bf16[32,1,4096]{2,0,1:T(8,128)(2,1)} %param.11) | copy-start | bytes 786436
  37.1 23.8 %copy-start.1 = (bf16[32,1,4096]{2,0,1:T(8,128)(2,1)S(1)}, bf16[32,1,4096]{2,0,1:T(8,128)(2,1)}, u32[]{:S(2)}) copy-start(bf16[32,1,4096]{2,0,1:T(8,128)(2,1)} %param.10) | copy-start | bytes 786436
  61.2 31.0 %copy-start.2 = (f32[1,4096]{1,0:T(1,128)S(1)}, f32[1,4096]{1,0:T(1,128)}, u32[]{:S(2)}) copy-start(f32[1,4096]{1,0:T(1,128)} %param.17) | copy-start | bytes 49156
  189.1 3.6 %copy-start.3 = (s32[4]{0:T(128)S(1)}, s32[4]{0:T(128)}, u32[]{:S(2)}) copy-start(s32[4]{0:T(128)} %param.13) | copy-start | bytes 52
  189.1 30.2 %all-to-all-start.1 = ((bf16[4,32,4096]{2,1,0:T(8,128)(2,1)}), bf16[4,32,4096]{2,1,0:T(8,128)(2,1)S(1)}, u32[]{:S(2)}, u32[]{:S(2)}) async-start(bf16[4,32,4096]{2,1,0:T(8,128)(2,1)} %bitcast.13), calls=%async_computation.1 | async-start | bytes 2097152 | tf_op jit(solution)/shard_map/all_to_all | solution.py:443
